TPU v7x, 32 devices: a whole 2x2x4 slice. The times are simulated.
32 devices in a mesh: dp: 16 (over z, y, x), mp: 2 (over core).
Axes of the slice: x: 2, y: 2, z: 4, core: 2. Of those that a mesh axis runs over, the one named last changes fastest.
Arguments:
- tokens_in: bfloat16 [65536, 1024], P('dp'), may hold values from -6 to 6
- route_mask: int32 [65536], P('dp'), may hold values from 0 to 1, as said below
- cotangent: bfloat16 [65536, 1024], P('dp'), may hold values from -6 to 6
- w_query: bfloat16 [1024, 1024], P('dp', 'mp'), may hold values from -0.1875 to 0.1875
- w_key: bfloat16 [1024, 1024], P('dp', 'mp'), may hold values from -0.1875 to 0.1875
- w_value: bfloat16 [1024, 1024], P('dp', 'mp'), may hold values from -0.1875 to 0.1875
- w_out: bfloat16 [1024, 1024], P('mp', 'dp'), may hold values from -1 to 1
- w_up: bfloat16 [1024, 4096], P('dp', 'mp'), may hold values from -0.1875 to 0.1875
- w_down: bfloat16 [4096, 1024], P('mp', 'dp'), may hold values from -0.1875 to 0.1875
- gain_attn: bfloat16 [1024], P('dp'), may hold values from 0.099609375 to 1.8984375
- gain_mlp: bfloat16 [1024], P('dp'), may hold values from 0.099609375 to 1.8984375
- router: bfloat16 [1024], P('dp'), may hold values from -0.1875 to 0.1875
Outputs:
- block_out: bfloat16 [65536, 1024], P('dp')
- input_grad: bfloat16 [65536, 1024], P('dp')
- grad_query: float32 [1024, 1024], P('dp', 'mp')
- grad_key: float32 [1024, 1024], P('dp', 'mp')
- grad_value: float32 [1024, 1024], P('dp', 'mp')
- grad_out: float32 [1024, 1024], P('mp', 'dp')
- grad_up: float32 [1024, 4096], P('dp', 'mp')
- grad_down: float32 [4096, 1024], P('mp', 'dp')
- grad_gain_attn: float32 [1024], P('dp')
- grad_gain_mlp: float32 [1024], P('dp')
- grad_router: float32 [1024], P('dp')
- routed_share: float32 [], replicated
- gate_mean: float32 [], replicated
Inputs may be any that keep to these rules, and one draw needn't show every extreme that they name: `route_mask`: sequence s holds tokens s * 2048 to (s + 1) * 2048 - 1. Every sequence has 1 to 256 routed tokens, and some sequence has exactly 256. For every i below 16, the routed counts of sequence 2 i and of sequence 2 j + 1, where j is i with the highest bit of 15 flipped, add up to at most 320, exactly 320 for some i.
All inputs are finite; a program needn't handle non-finite values.
Results may differ from a plain program's by a relative error of at most 0.018.
Values may be sent and summed in bfloat16 or wider, within the bound.
No kernel may reach another device: no remote copies, remote signals or barrier semaphores. Data moves between devices by JAX's collectives and lax.ppermute only.
A program may use at most 192 MiB of HBM per device.

v0:
```python
import jax
import jax.numpy as jnp
from jax import lax
from jax.sharding import PartitionSpec as P

HD = 64
LEN = 2048
SEQ_DEV = 2
CAP = 256


epsilon = 1e-06
negative = -1e30


def matmul(left_side, right_side):
    return jnp.dot(left_side, right_side, preferred_element_type=jnp.float32)


def compact(sequence, selected):
    slot_index = jnp.nonzero(selected, size=CAP, fill_value=LEN)[0].astype(jnp.int32)
    picked = jnp.take(sequence, slot_index, axis=0, mode="fill", fill_value=0)
    return (picked, slot_index)


def norm_back(upstream, normal, inverse, gain_row):
    scaled = upstream * gain_row
    return inverse * (scaled - normal * jnp.mean(scaled * normal, axis=-1, keepdims=True))


def block_forward(routed, segment, usable, weights_full):
    w_query, w_key, w_value, w_out, w_up, w_down, gain_one, gain_two, router = weights_full
    row_count = routed.shape[0]
    local_heads = w_query.shape[1] // HD
    score_scale = HD ** (-0.5)
    inputs = routed.astype(jnp.float32)
    gate_value = jax.nn.sigmoid(matmul(routed, router))
    inverse_one = lax.rsqrt(jnp.mean(inputs * inputs, axis=-1, keepdims=True) + epsilon)
    normal_one = inputs * inverse_one
    normed = (normal_one * gain_one.astype(jnp.float32)).astype(jnp.bfloat16)
    queries = matmul(normed, w_query).astype(jnp.bfloat16).reshape(row_count, local_heads, HD)
    key_heads = matmul(normed, w_key).astype(jnp.bfloat16).reshape(row_count, local_heads, HD)
    value_heads = matmul(normed, w_value).astype(jnp.bfloat16).reshape(row_count, local_heads, HD)
    position = jnp.arange(row_count)
    allowed = (
        (position[None, :] <= position[:, None])
        & (segment[None, :] == segment[:, None])
        & usable[None, :]
    )
    scores = (
        jnp.einsum("qhe,khe->hqk", queries, key_heads, preferred_element_type=jnp.float32)
        * score_scale
    )
    scores = jnp.where(allowed[None], scores, negative)
    probability = jax.nn.softmax(scores, axis=-1)
    probability_low = probability.astype(jnp.bfloat16)
    attended = jnp.einsum(
        "hqk,khe->qhe", probability_low, value_heads, preferred_element_type=jnp.float32
    )
    attended = attended.astype(jnp.bfloat16).reshape(row_count, local_heads * HD)
    attention = lax.psum(matmul(attended, w_out).astype(jnp.bfloat16), "mp").astype(jnp.float32)
    residual = inputs + attention
    inverse_two = lax.rsqrt(jnp.mean(residual * residual, axis=-1, keepdims=True) + epsilon)
    normal_two = residual * inverse_two
    normed_two = (normal_two * gain_two.astype(jnp.float32)).astype(jnp.bfloat16)
    hidden = matmul(normed_two, w_up)
    active = jax.nn.gelu(hidden).astype(jnp.bfloat16)
    feed_out = lax.psum(matmul(active, w_down).astype(jnp.bfloat16), "mp").astype(jnp.float32)
    branch = attention + feed_out
    output = (inputs + gate_value[:, None] * branch).astype(jnp.bfloat16)
    stored = (
        inputs,
        gate_value,
        branch,
        inverse_one,
        normal_one,
        normed,
        queries,
        key_heads,
        value_heads,
        probability,
        probability_low,
        attended,
        inverse_two,
        normal_two,
        normed_two,
        hidden,
        active,
    )
    return (output, stored)


def block_backward(upstream_rows, stored, weights_full):
    w_query, w_key, w_value, w_out, w_up, w_down, gain_one, gain_two, router = weights_full
    (
        inputs,
        gate_value,
        branch,
        inverse_one,
        normal_one,
        normed,
        queries,
        key_heads,
        value_heads,
        probability,
        probability_low,
        attended,
        inverse_two,
        normal_two,
        normed_two,
        hidden,
        active,
    ) = stored
    row_count = inputs.shape[0]
    score_scale = HD ** (-0.5)
    upstream = upstream_rows.astype(jnp.float32)
    d_logit = jnp.sum(upstream * branch, axis=-1) * gate_value * (1.0 - gate_value)
    d_router = jnp.sum(d_logit[:, None] * inputs, axis=0)
    d_branch = gate_value[:, None] * upstream
    d_feed = d_branch.astype(jnp.bfloat16)
    grad_down = matmul(active.T, d_feed)
    d_active = matmul(d_feed, w_down.T)
    gelu_value, gelu_back = jax.vjp(jax.nn.gelu, hidden)
    d_hidden = gelu_back(d_active)[0].astype(jnp.bfloat16)
    grad_up = matmul(normed_two.T, d_hidden)
    d_normed_two = matmul(d_hidden, w_up.T)
    part_inner = norm_back(d_normed_two, normal_two, inverse_two, gain_two.astype(jnp.float32))
    part_gain_two = jnp.sum(d_normed_two * normal_two, axis=0)
    d_inner, grad_gain_two = (
        lax.psum(part_inner.astype(jnp.bfloat16), "mp").astype(jnp.float32),
        lax.psum(part_gain_two.astype(jnp.bfloat16), "mp").astype(jnp.float32),
    )
    mlp_terms = (grad_up, grad_down, grad_gain_two, d_router)
    d_attention = (d_branch + d_inner).astype(jnp.bfloat16)
    grad_out = matmul(attended.T, d_attention)
    d_attended = matmul(d_attention, w_out.T).astype(jnp.bfloat16).reshape(queries.shape)
    d_probability = jnp.einsum(
        "qhe,khe->hqk", d_attended, value_heads, preferred_element_type=jnp.float32
    )
    d_values = jnp.einsum(
        "hqk,qhe->khe", probability_low, d_attended, preferred_element_type=jnp.float32
    )
    d_values = d_values.astype(jnp.bfloat16).reshape(row_count, -1)
    d_scores = probability * (
        d_probability - jnp.sum(probability * d_probability, axis=-1, keepdims=True)
    )
    d_scores = d_scores.astype(jnp.bfloat16)
    d_queries = (
        jnp.einsum("hqk,khe->qhe", d_scores, key_heads, preferred_element_type=jnp.float32)
        * score_scale
    )
    d_queries = d_queries.astype(jnp.bfloat16).reshape(row_count, -1)
    d_keys = (
        jnp.einsum("hqk,qhe->khe", d_scores, queries, preferred_element_type=jnp.float32)
        * score_scale
    )
    d_keys = d_keys.astype(jnp.bfloat16).reshape(row_count, -1)
    grad_query = matmul(normed.T, d_queries)
    grad_key = matmul(normed.T, d_keys)
    grad_value = matmul(normed.T, d_values)
    d_normed = matmul(d_queries, w_query.T) + matmul(d_keys, w_key.T) + matmul(d_values, w_value.T)
    part_input = norm_back(d_normed, normal_one, inverse_one, gain_one.astype(jnp.float32))
    part_gain_one = jnp.sum(d_normed * normal_one, axis=0)
    d_norm_input, grad_gain_one = (
        lax.psum(part_input.astype(jnp.bfloat16), "mp").astype(jnp.float32),
        lax.psum(part_gain_one.astype(jnp.bfloat16), "mp").astype(jnp.float32),
    )
    d_rows = upstream + d_inner + d_logit[:, None] * router.astype(jnp.float32) + d_norm_input
    attn_terms = (grad_query, grad_key, grad_value, grad_out, grad_gain_one)
    return (d_rows.astype(jnp.bfloat16), attn_terms, mlp_terms)


def body(
    tokens_in,
    route_mask,
    cotangent,
    w_query,
    w_key,
    w_value,
    w_out,
    w_up,
    w_down,
    gain_attn,
    gain_mlp,
    router,
):
    shards = (w_query, w_key, w_value, w_out, w_up, w_down, gain_attn, gain_mlp, router)
    weights_full = (
        lax.all_gather(shards[0], "dp", axis=0, tiled=True),
        lax.all_gather(shards[1], "dp", axis=0, tiled=True),
        lax.all_gather(shards[2], "dp", axis=0, tiled=True),
        lax.all_gather(shards[3], "dp", axis=1, tiled=True),
        lax.all_gather(shards[4], "dp", axis=0, tiled=True),
        lax.all_gather(shards[5], "dp", axis=1, tiled=True),
        lax.all_gather(shards[6], "dp", axis=0, tiled=True),
        lax.all_gather(shards[7], "dp", axis=0, tiled=True),
        lax.all_gather(shards[8], "dp", axis=0, tiled=True),
    )
    width = tokens_in.shape[1]
    sequences = tokens_in.reshape(SEQ_DEV, LEN, width)
    selection = route_mask.reshape(SEQ_DEV, LEN)
    upstream_all = cotangent.reshape(SEQ_DEV, LEN, width)
    routed_first, slots_first = compact(sequences[0], selection[0])
    routed_second, slots_second = compact(sequences[1], selection[1])
    grads_first = jnp.take(upstream_all[0], slots_first, axis=0, mode="fill", fill_value=0)
    grads_second = jnp.take(upstream_all[1], slots_second, axis=0, mode="fill", fill_value=0)
    count_first = jnp.sum(selection[0])
    count_second = jnp.sum(selection[1])
    position = jnp.arange(CAP)
    routed = jnp.concatenate([routed_first, routed_second], axis=0)
    segment = jnp.repeat(jnp.arange(2, dtype=jnp.int32), CAP)
    usable = jnp.concatenate([position < count_first, position < count_second])
    output, stored = block_forward(routed, segment, usable, weights_full)
    result_first = output[:CAP]
    result_second = output[CAP:]
    upstream_rows = jnp.concatenate([grads_first, grads_second], axis=0)
    weights_back = (
        lax.all_gather(shards[0], "dp", axis=0, tiled=True),
        lax.all_gather(shards[1], "dp", axis=0, tiled=True),
        lax.all_gather(shards[2], "dp", axis=0, tiled=True),
        lax.all_gather(shards[3], "dp", axis=1, tiled=True),
        lax.all_gather(shards[4], "dp", axis=0, tiled=True),
        lax.all_gather(shards[5], "dp", axis=1, tiled=True),
        lax.all_gather(shards[6], "dp", axis=0, tiled=True),
        lax.all_gather(shards[7], "dp", axis=0, tiled=True),
        lax.all_gather(shards[8], "dp", axis=0, tiled=True),
    )
    d_rows, attn_terms, mlp_terms = block_backward(upstream_rows, stored, weights_back)
    d_first = d_rows[:CAP]
    d_second = d_rows[CAP:]
    block_out = jnp.stack(
        [
            sequences[0].at[slots_first].set(result_first, mode="drop"),
            sequences[1].at[slots_second].set(result_second, mode="drop"),
        ]
    ).reshape(-1, width)
    input_grad = jnp.stack(
        [
            upstream_all[0].at[slots_first].set(d_first, mode="drop"),
            upstream_all[1].at[slots_second].set(d_second, mode="drop"),
        ]
    ).reshape(-1, width)
    summed = (
        lax.psum_scatter(attn_terms[0], "dp", scatter_dimension=0, tiled=True),
        lax.psum_scatter(attn_terms[1], "dp", scatter_dimension=0, tiled=True),
        lax.psum_scatter(attn_terms[2], "dp", scatter_dimension=0, tiled=True),
        lax.psum_scatter(attn_terms[3], "dp", scatter_dimension=1, tiled=True),
        lax.psum_scatter(mlp_terms[0], "dp", scatter_dimension=0, tiled=True),
        lax.psum_scatter(mlp_terms[1], "dp", scatter_dimension=1, tiled=True),
        lax.psum_scatter(attn_terms[4], "dp", scatter_dimension=0, tiled=True),
        lax.psum_scatter(mlp_terms[2], "dp", scatter_dimension=0, tiled=True),
        lax.psum_scatter(mlp_terms[3], "dp", scatter_dimension=0, tiled=True),
    )
    gate_total = jnp.sum(jnp.where(usable, stored[1], 0.0))
    routed_total, gate_sum = lax.psum((jnp.sum(usable.astype(jnp.float32)), gate_total), "dp")
    token_total = tokens_in.shape[0] * lax.axis_size("dp")
    return (
        block_out,
        input_grad,
        summed[0],
        summed[1],
        summed[2],
        summed[3],
        summed[4],
        summed[5],
        summed[6],
        summed[7],
        summed[8],
        routed_total / token_total,
        gate_sum / routed_total,
    )


def solution(mesh):
    return jax.shard_map(
        body,
        mesh=mesh,
        in_specs=(
            P("dp", None),
            P("dp"),
            P("dp", None),
            P("dp", "mp"),
            P("dp", "mp"),
            P("dp", "mp"),
            P("mp", "dp"),
            P("dp", "mp"),
            P("mp", "dp"),
            P("dp"),
            P("dp"),
            P("dp"),
        ),
        out_specs=(
            P("dp", None),
            P("dp", None),
            P("dp", "mp"),
            P("dp", "mp"),
            P("dp", "mp"),
            P("mp", "dp"),
            P("dp", "mp"),
            P("mp", "dp"),
            P("dp"),
            P("dp"),
            P("dp"),
            P(),
            P(),
        ),
        check_vma=False,
    )
```

profile of v0, /device:TPU:10, one launch (start us, length us, event | category | flops | bytes accessed | tf_op | source)
XLA Modules:
  0.0 1213.4 jit_solution(6419622818406484618)
XLA Ops:
  14.6 31.8 %all-reduce.7 = (bf16[1024]{0:T(1024)(128)(2,1)S(1)}, bf16[1024]{0:T(1024)(128)(2,1)S(1)}, bf16[1024]{0:T(1024)(128)(2,1)S(1)}) all-reduce(bf16[1024]{0:T(1024)(128)(2,1)S(1)} %dynamic-update-slice.1, bf16[1024]{0:T(1024)(128)(2,1)S(1)} %dynamic-update-slice.2, ...), channel_id=1, replica_groups=mesh['dp'=16,'mp'=2] {'dp'}, use_global_device_ids=true, to_apply=%add.1 | all-reduce | flops 3072 | bytes 12288
  48.7 14.7 %scatter_custom_fusion = s32[256]{0:T(256)S(1)} fusion(s32[2048]{0:T(1024)S(1)} %bitcast.114, s32[2048]{0:T(1024)S(1)} %broadcast.353, s32[]{:T(128)} %constant.90.clone.1), kind=kCustom, calls=%fused_computation.164 | custom fusion | flops 2048 | bytes 1028 | tf_op jit(solution)/shard_map/scatter-add | solution.py:21
  65.0 14.8 %scatter_custom_fusion.1 = s32[256]{0:T(256)S(1)} fusion(s32[2048]{0:T(1024)S(1)} %bitcast.115, s32[2048]{0:T(1024)S(1)} %broadcast.353, s32[]{:T(128)} %constant.90.clone.1), kind=kCustom, calls=%fused_computation.162 | custom fusion | flops 2048 | bytes 1028 | tf_op jit(solution)/shard_map/scatter-add | solution.py:21
  115.4 8.0 all-gather.9.cloned.1.call-done
  125.4 54.8 %all-gather.7.cloned.1.call-done = bf16[1024,512]{1,0:T(8,128)(2,1)} async-done(((bf16[64,512]{1,0:T(8,128)(2,1)}), bf16[1024,512]{1,0:T(8,128)(2,1)}) %all-gather.7.cloned.1.call-update) | async-done | bytes 1048592 | tf_op jit(solution)/shard_map/all_gather | solution.py:191
  193.3 43.7 %all-gather.13.cloned.1.call-done = bf16[512,1024]{0,1:T(8,128)(2,1)} async-done(((bf16[512,64]{0,1:T(8,128)(2,1)}), bf16[512,1024]{0,1:T(8,128)(2,1)}) %all-gather.13.cloned.1.call-update) | async-done | bytes 1048592 | tf_op jit(solution)/shard_map/all_gather | solution.py:192
  241.4 18.4 %all-reduce.14.cloned.1.call-done = bf16[512,1024]{1,0:T(8,128)(2,1)} async-done(((bf16[512,1024]{1,0:T(8,128)(2,1)}), bf16[512,1024]{1,0:T(8,128)(2,1)}) %all-reduce.14.cloned.1.call-update) | async-done | bytes 1048592 | tf_op jit(solution)/shard_map/psum | solution.py:61
  261.5 78.3 %all-gather.15.cloned.1.call-done = bf16[1024,2048]{1,0:T(8,128)(2,1)} async-done(((bf16[64,2048]{1,0:T(8,128)(2,1)}), bf16[1024,2048]{1,0:T(8,128)(2,1)}) %all-gather.15.cloned.1.call-update) | async-done | bytes 4194320 | tf_op jit(solution)/shard_map/all_gather | solution.py:193
  346.4 71.2 %all-gather.17.cloned.1.call-done = bf16[2048,1024]{0,1:T(8,128)(2,1)} async-done(((bf16[2048,64]{0,1:T(8,128)(2,1)}), bf16[2048,1024]{0,1:T(8,128)(2,1)}) %all-gather.17.cloned.1.call-update) | async-done | bytes 4194320 | tf_op jit(solution)/shard_map/all_gather | solution.py:194
  417.6 7.1 convolution_convert_fusion.1
  424.8 9.2 fusion.8
  434.1 9.4 all-reduce.16.cloned.1.call-done
  443.4 7.2 multiply_reduce_fusion.1
  452.4 20.9 %all-reduce.18.cloned.1.call-done = bf16[512,1024]{1,0:T(8,128)(2,1)} async-done(((bf16[512,1024]{1,0:T(8,128)(2,1)}), bf16[512,1024]{1,0:T(8,128)(2,1)}) %all-reduce.18.cloned.1.call-update) | async-done | bytes 1048592 | tf_op jit(solution)/shard_map/psum | solution.py:130
  507.8 8.0 fusion.56
  515.8 7.4 fusion.75
  538.6 7.7 pad_maximum_fusion
  548.8 66.0 %all-reduce.6 = (f32[1024]{0:T(1024)S(1)}, f32[1024]{0:T(1024)S(1)}, f32[1024]{0:T(1024)S(1)}, f32[]{:T(128)}, f32[]{:T(128)}) all-reduce(bf16[1024]{0:T(1024)(128)(2,1)S(1)} %get-tuple-element.32, bf16[1024]{0:T(1024)(128)(2,1)S(1)} %get-tuple-element.33, ...), channel_id=8, replica_groups=mesh['dp'=16,'mp'=2] {'dp'}, use_global_device_ids=true, to_apply=%region_38.40.clone | all-reduce | flops 3074 | bytes 20496
  633.4 7.6 pad_maximum_fusion.1
  641.0 28.6 %reduce-scatter.11.cloned.1.call-done = f32[64,512]{1,0:T(8,128)} async-done(((f32[1024,512]{1,0:T(8,128)}), f32[64,512]{1,0:T(8,128)}) %reduce-scatter.11.cloned.1.call-update) | async-done | bytes 131088 | tf_op jit(solution)/shard_map/reduce_scatter | solution.py:246
  669.7 81.1 %reduce-scatter.7.cloned.1.call-done = f32[64,512]{1,0:T(8,128)} async-done(((f32[1024,512]{1,0:T(8,128)}), f32[64,512]{1,0:T(8,128)}) %reduce-scatter.7.cloned.1.call-update) | async-done | bytes 131088 | tf_op jit(solution)/shard_map/reduce_scatter | solution.py:244
  750.7 80.3 %reduce-scatter.9.cloned.1.call-done = f32[64,512]{1,0:T(8,128)} async-done(((f32[1024,512]{1,0:T(8,128)}), f32[64,512]{1,0:T(8,128)}) %reduce-scatter.9.cloned.1.call-update) | async-done | bytes 131088 | tf_op jit(solution)/shard_map/reduce_scatter | solution.py:245
  831.0 190.3 %reduce-scatter.17.cloned.1.call-done = f32[2048,64]{0,1:T(8,128)} async-done(((f32[2048,1024]{0,1:T(8,128)}), f32[2048,64]{0,1:T(8,128)}) %reduce-scatter.17.cloned.1.call-update) | async-done | bytes 524304 | tf_op jit(solution)/shard_map/reduce_scatter | solution.py:249
  1021.4 183.0 %reduce-scatter.15.cloned.1.call-done = f32[64,2048]{1,0:T(8,128)} async-done(((f32[1024,2048]{1,0:T(8,128)}), f32[64,2048]{1,0:T(8,128)}) %reduce-scatter.15.cloned.1.call-update) | async-done | bytes 524304 | tf_op jit(solution)/shard_map/reduce_scatter | solution.py:248
  (162 shorter events, 143.6 us)
Async XLA Ops:
  7.2 106.1 %all-gather.11.cloned.1.call-start = ((), (), s32[]{:S(2)}) async-start(), calls=%async_computation.8 | async-start | bytes 1114112 | tf_op jit(solution)/shard_map/all_gather | solution.py:190
  7.9 115.5 %all-gather.9.cloned.1.call-start = ((), (), s32[]{:S(2)}) async-start(), calls=%async_computation.7 | async-start | bytes 1114112 | tf_op jit(solution)/shard_map/all_gather | solution.py:189
  8.7 171.6 %all-gather.7.cloned.1.call-start = ((), (), s32[]{:S(2)}) async-start(), calls=%async_computation.6 | async-start | bytes 1114112 | tf_op jit(solution)/shard_map/all_gather | solution.py:191
  9.4 227.6 %all-gather.13.cloned.1.call-start = ((), (), s32[]{:S(2)}) async-start(), calls=%async_computation.9 | async-start | bytes 1114112 | tf_op jit(solution)/shard_map/all_gather | solution.py:192
  10.0 249.8 %all-reduce.14.cloned.1.call-start = ((), (), s32[]{:S(2)}) async-start(), calls=%async_computation.10 | async-start | bytes 2097152 | tf_op jit(solution)/shard_map/psum | solution.py:61
  115.4 67.8 %copy-start.9 = (bf16[512,512]{0,1:T(8,128)(2,1)}, bf16[512,512]{0,1:T(8,128)(2,1)S(1)}, u32[]{:S(2)}) copy-start(bf16[512,512]{0,1:T(8,128)(2,1)S(1)} %convolution_convert_fusion.3) | copy-start | bytes 1572868
  125.4 57.7 %copy-start.11 = (bf16[512,512]{0,1:T(8,128)(2,1)}, bf16[512,512]{0,1:T(8,128)(2,1)S(1)}, u32[]{:S(2)}) copy-start(bf16[512,512]{0,1:T(8,128)(2,1)S(1)} %convolution_convert_fusion.4) | copy-start | bytes 1572868
  193.3 47.3 %copy-start.4 = (bf16[8,64,512]{2,1,0:T(8,128)(2,1)}, bf16[8,64,512]{2,1,0:T(8,128)(2,1)S(1)}, u32[]{:S(2)}) copy-start(bf16[8,64,512]{2,1,0:T(8,128)(2,1)S(1)} %fusion.36) | copy-start | bytes 1572868
  240.0 99.8 %all-gather.15.cloned.1.call-start = ((), (), s32[]{:S(2)}) async-start(), calls=%async_computation.11 | async-start | bytes 4456448 | tf_op jit(solution)/shard_map/all_gather | solution.py:193
  240.6 177.1 %all-gather.17.cloned.1.call-start = ((), (), s32[]{:S(2)}) async-start(), calls=%async_computation.12 | async-start | bytes 4456448 | tf_op jit(solution)/shard_map/all_gather | solution.py:194
  241.3 202.1 %all-reduce.16.cloned.1.call-start = ((), (), s32[]{:S(2)}) async-start(), calls=%async_computation.13 | async-start | bytes 2097152 | tf_op jit(solution)/shard_map/psum | solution.py:68
  259.8 80.0 %copy-start = (bf16[512,1024]{1,0:T(8,128)(2,1)S(1)}, bf16[512,1024]{1,0:T(8,128)(2,1)}, u32[]{:S(2)}) copy-start(bf16[512,1024]{1,0:T(8,128)(2,1)} %all-reduce.14.cloned.1.call-done) | copy-start | bytes 3145732
  424.8 48.5 %all-reduce.18.cloned.1.call-start = ((), (), s32[]{:S(2)}) async-start(), calls=%async_computation.14 | async-start | bytes 2097152 | tf_op jit(solution)/shard_map/psum | solution.py:130
  452.4 166.2 %all-reduce.20.cloned.1.call-start = ((), (), s32[]{:S(2)}) async-start(), calls=%async_computation.15 | async-start | bytes 2097152 | tf_op jit(solution)/shard_map/psum | solution.py:165
  473.3 7.6 slice-start
  475.9 5.0 slice-start.1
  480.9 9.3 copy-start.13
  493.7 147.4 %reduce-scatter.13.cloned.1.call-start = ((), (), s32[]{:S(2)}) async-start(), calls=%async_computation.19 | async-start | bytes 2228224 | tf_op jit(solution)/shard_map/reduce_scatter | solution.py:247
  497.4 172.3 %reduce-scatter.11.cloned.1.call-start = ((), (), s32[]{:S(2)}) async-start(), calls=%async_computation.18 | async-start | bytes 2228224 | tf_op jit(solution)/shard_map/reduce_scatter | solution.py:246
  500.8 250.0 %reduce-scatter.7.cloned.1.call-start = ((), (), s32[]{:S(2)}) async-start(), calls=%async_computation.16 | async-start | bytes 2228224 | tf_op jit(solution)/shard_map/reduce_scatter | solution.py:244
  504.1 326.9 %reduce-scatter.9.cloned.1.call-start = ((), (), s32[]{:S(2)}) async-start(), calls=%async_computation.17 | async-start | bytes 2228224 | tf_op jit(solution)/shard_map/reduce_scatter | solution.py:245
  507.5 513.8 %reduce-scatter.17.cloned.1.call-start = ((), (), s32[]{:S(2)}) async-start(), calls=%async_computation.21 | async-start | bytes 8912896 | tf_op jit(solution)/shard_map/reduce_scatter | solution.py:249
  515.8 688.6 %reduce-scatter.15.cloned.1.call-start = ((), (), s32[]{:S(2)}) async-start(), calls=%async_computation.20 | async-start | bytes 8912896 | tf_op jit(solution)/shard_map/reduce_scatter | solution.py:248
  538.6 79.9 %copy-start.1 = (bf16[512,1024]{1,0:T(8,128)(2,1)S(1)}, bf16[512,1024]{1,0:T(8,128)(2,1)}, u32[]{:S(2)}) copy-start(bf16[512,1024]{1,0:T(8,128)(2,1)} %all-reduce.18.cloned.1.call-done) | copy-start | bytes 3145732
  (9 other events, 18.3 us)
Sparse Core Ops, SparseCore 0:
  10.8 55.5 all-gather.10
  69.2 54.1 all-gather.8
  126.1 54.1 all-gather.6
  182.9 54.0 all-gather.12
  240.1 19.6 all-reduce.13
  262.8 76.9 all-gather.14
  342.9 74.6 all-gather.16
  424.9 18.4 all-reduce.15
  452.5 20.7 all-reduce.17
  493.8 20.7 all-reduce.19
  517.4 72.4 reduce-scatter.12
  592.6 76.9 reduce-scatter.10
  672.5 78.1 reduce-scatter.6
  753.4 77.5 reduce-scatter.8
  833.7 187.5 reduce-scatter.16
  1024.1 180.2 reduce-scatter.14
where the time goes:
time: 1220 us; the launch traced here: 1210 us
  waiting for transfers between devices  872 us (71%)
  blocking collectives  100 us (8%)
  matrix products  94.6 us (8%)
  local copies, waits for them, and re-layouts  62.9 us (5%)
  other arithmetic  62.6 us (5%)
  between operations  20.4 us (2%)
    reduce_scatter x1, waiting for transfers between devices, body(): lax.psum_scatter(mlp_terms[1], 'dp', scatter_dimension=1, tiled=True)  190 us
    reduce_scatter x1, waiting for transfers between devices, body(): lax.psum_scatter(mlp_terms[0], 'dp', scatter_dimension=0, tiled=True)  183 us
    unnamed x2, blocking collectives  97.7 us
    reduce_scatter x1, waiting for transfers between devices, body(): lax.psum_scatter(attn_terms[0], 'dp', scatter_dimension=0, tiled=True)  81.1 us
    reduce_scatter x1, waiting for transfers between devices, body(): lax.psum_scatter(attn_terms[1], 'dp', scatter_dimension=0, tiled=True)  80.3 us
    all_gather x1, waiting for transfers between devices, body(): lax.all_gather(shards[4], 'dp', axis=0, tiled=True)  78.3 us
    dot_general x19, matrix products, matmul(): return jnp.dot(left_side, right_side, preferred_element_type=jnp.float32)  75.1 us
    all_gather x1, waiting for transfers between devices, body(): lax.all_gather(shards[5], 'dp', axis=1, tiled=True)  71.2 us
  transfers between devices with their start and end apart: 16, of which 13 were waited for; matrix products, arithmetic and copies ran while one was open for 15% of the time, Pallas kernels for 0%

commit v1 on v0

v1 whole, which is shorter than its diff:
```python
import functools
import jax
import jax.numpy as jnp
from jax import lax
from jax.experimental import pallas as pl
from jax.experimental.pallas import tpu as pltpu
from jax.sharding import PartitionSpec as P

HD = 64
LEN = 2048
CAP = 256

epsilon = 1e-06
negative = -1e30
BF = jnp.bfloat16
F32 = jnp.float32


def matmul(left_side, right_side):
    return jnp.dot(left_side, right_side, preferred_element_type=F32)


def matmul_nt(left_side, right_side):
    return lax.dot_general(left_side, right_side, (((1,), (1,)), ((), ())), preferred_element_type=F32)


def bit_orders(n):
    bits = n.bit_length() - 1
    if bits == 4:
        x, y, z1, z2 = 1, 2, 4, 8
        first = ((z2, z1, x, y), (z2, z1, y, x))
        second = ((x, z2, z1, y), (y, z2, z1, x))
        return (first, second, second)
    down = tuple(1 << b for b in reversed(range(bits)))
    return ((down, down),) * 3


def pairs(n, one, two):
    return [(d * 2 + c, (d ^ (one, two)[c]) * 2 + c) for d in range(n) for c in range(2)]


def block_ids(n, orders):
    me = lax.axis_index("dp")
    core = lax.axis_index("mp")
    tables = []
    for order in orders:
        table = [0]
        for bit in order:
            table = table + [t ^ bit for t in table]
        tables.append(table)
    return me ^ jnp.where(core == 0, jnp.array(tables[0], jnp.int32), jnp.array(tables[1], jnp.int32))


def gather(shard, n, orders):
    held = shard
    for one, two in zip(*orders):
        got = lax.ppermute(held, ("dp", "mp"), pairs(n, one, two))
        held = jnp.concatenate([held, got], axis=0)
    return held


def scatter_sum(ordered, n, orders):
    held = ordered
    steps = list(zip(*orders))[::-1]
    for at, (one, two) in enumerate(steps):
        half = held.shape[0] // 2
        got = lax.ppermute(held[half:], ("dp", "mp"), pairs(n, one, two))
        held = held[:half].astype(F32) + got.astype(F32)
        if at < len(steps) - 1:
            held = held.astype(BF)
    return held


def reorder_kernel(ids_ref, in_ref, out_ref):
    out_ref[...] = in_ref[...].astype(out_ref.dtype)


def reorder(array, ids, n, inverse):
    rows, width = array.shape
    step = rows // n
    if step % 16:
        blocks = array.reshape(n, step, width)
        if inverse:
            blocks = jnp.zeros_like(blocks).at[ids].set(blocks)
        else:
            blocks = blocks[ids]
        return blocks.reshape(rows, width).astype(BF)
    here = lambda i, ids_ref: (i, 0)
    there = lambda i, ids_ref: (ids_ref[i], 0)
    return pl.pallas_call(
        reorder_kernel,
        grid_spec=pltpu.PrefetchScalarGridSpec(
            num_scalar_prefetch=1,
            grid=(n,),
            in_specs=[pl.BlockSpec((step, width), here if inverse else there)],
            out_specs=pl.BlockSpec((step, width), there if inverse else here),
        ),
        out_shape=jax.ShapeDtypeStruct((rows, width), BF),
        cost_estimate=pl.CostEstimate(flops=0, bytes_accessed=4 * rows * width, transcendentals=0),
    )(ids, array)


def compact(sequence, selected):
    slot_index = jnp.nonzero(selected, size=CAP, fill_value=LEN)[0].astype(jnp.int32)
    picked = jnp.take(sequence, slot_index, axis=0, mode="fill", fill_value=0)
    return (picked, slot_index)


def swap_sum(part):
    low = part.astype(BF)
    other = lax.ppermute(low, "mp", [(0, 1), (1, 0)])
    return low.astype(F32) + other.astype(F32)


def body(
    tokens_in,
    route_mask,
    cotangent,
    w_query,
    w_key,
    w_value,
    w_out,
    w_up,
    w_down,
    gain_attn,
    gain_mlp,
    router,
):
    n = lax.axis_size("dp")
    orders = bit_orders(n)
    ids = [block_ids(n, o) for o in orders]
    mine = w_query.shape[0]
    heads_width = w_query.shape[1]
    width = tokens_in.shape[1]
    seqs = tokens_in.shape[0] // LEN
    extras = jnp.concatenate(
        [gain_attn[:, None], gain_mlp[:, None], router[:, None], jnp.zeros((mine, 125), BF)], axis=1
    )
    shard_attn = jnp.concatenate([w_query, w_key, w_value, w_out.T, extras], axis=1)
    full_attn = reorder(gather(shard_attn, n, orders[0]), ids[0], n, True)
    full_up = reorder(gather(w_up, n, orders[1]), ids[1], n, True)
    full_down = reorder(gather(w_down.T, n, orders[2]), ids[2], n, True)
    w = heads_width
    w_qkv = full_attn[:, : 3 * w]
    w_out_t = full_attn[:, 3 * w : 4 * w]
    vectors = full_attn[:, 4 * w :]
    gain_one = vectors[:, 0].astype(F32)
    gain_two = vectors[:, 1].astype(F32)
    router_all = vectors[:, 2]

    sequences = tokens_in.reshape(seqs, LEN, width)
    selection = route_mask.reshape(seqs, LEN)
    upstream_all = cotangent.reshape(seqs, LEN, width)
    picked = [compact(sequences[s], selection[s]) for s in range(seqs)]
    slots = [p[1] for p in picked]
    routed = jnp.concatenate([p[0] for p in picked], axis=0)
    upstream_rows = jnp.concatenate(
        [jnp.take(upstream_all[s], slots[s], axis=0, mode="fill", fill_value=0) for s in range(seqs)], axis=0
    )
    counts = jnp.sum(selection, axis=1)
    position = jnp.arange(CAP)
    usable = position[None, :] < counts[:, None]
    allowed = (position[None, :] <= position[:, None])[None] & usable[:, None, :]
    rows = seqs * CAP
    local_heads = w // HD
    scale = HD ** (-0.5)

    inputs = routed.astype(F32)
    gate = jax.nn.sigmoid(matmul(routed, router_all))
    inverse_one = lax.rsqrt(jnp.mean(inputs * inputs, axis=-1, keepdims=True) + epsilon)
    normal_one = inputs * inverse_one
    normed = (normal_one * gain_one).astype(BF)
    qkv = matmul(normed, w_qkv).astype(BF).reshape(seqs, CAP, 3, local_heads, HD)
    queries, key_heads, value_heads = qkv[:, :, 0], qkv[:, :, 1], qkv[:, :, 2]
    scores = jnp.einsum("sqhe,skhe->shqk", queries, key_heads, preferred_element_type=F32) * scale
    scores = jnp.where(allowed[:, None], scores, negative)
    probability = jax.nn.softmax(scores, axis=-1)
    probability_low = probability.astype(BF)
    attended = jnp.einsum("shqk,skhe->sqhe", probability_low, value_heads, preferred_element_type=F32)
    attended = attended.astype(BF).reshape(rows, w)
    attention = swap_sum(matmul_nt(attended, w_out_t))
    residual = inputs + attention
    inverse_two = lax.rsqrt(jnp.mean(residual * residual, axis=-1, keepdims=True) + epsilon)
    normal_two = residual * inverse_two
    normed_two = (normal_two * gain_two).astype(BF)
    hidden = matmul(normed_two, full_up)
    active, gelu_back = jax.vjp(jax.nn.gelu, hidden)
    active = active.astype(BF)
    upstream = upstream_rows.astype(F32)
    d_branch = gate[:, None] * upstream
    d_feed = d_branch.astype(BF)
    grad_down = matmul(d_feed.T, active).astype(BF)
    sum_down = scatter_sum(reorder(grad_down, ids[2], n, False), n, orders[2])

    d_active = matmul(d_feed, full_down)
    d_hidden = gelu_back(d_active)[0].astype(BF)
    grad_up = matmul(normed_two.T, d_hidden).astype(BF)
    sum_up = scatter_sum(reorder(grad_up, ids[1], n, False), n, orders[1])
    d_normed_two = swap_sum(matmul_nt(d_hidden, full_up))
    scaled = d_normed_two * gain_two
    d_inner = inverse_two * (scaled - normal_two * jnp.mean(scaled * normal_two, axis=-1, keepdims=True))
    grad_gain_two = jnp.sum(d_normed_two * normal_two, axis=0)
    d_attention = (d_branch + d_inner).astype(BF)
    grad_out = matmul(d_attention.T, attended).astype(BF)
    d_attended = matmul(d_attention, w_out_t).astype(BF).reshape(seqs, CAP, local_heads, HD)
    d_probability = jnp.einsum("sqhe,skhe->shqk", d_attended, value_heads, preferred_element_type=F32)
    d_values = jnp.einsum("shqk,sqhe->skhe", probability_low, d_attended, preferred_element_type=F32)
    d_scores = probability * (d_probability - jnp.sum(probability * d_probability, axis=-1, keepdims=True))
    d_scores = d_scores.astype(BF)
    d_queries = jnp.einsum("shqk,skhe->sqhe", d_scores, key_heads, preferred_element_type=F32) * scale
    d_keys = jnp.einsum("shqk,sqhe->skhe", d_scores, queries, preferred_element_type=F32) * scale
    d_qkv = jnp.concatenate(
        [d_queries.astype(BF).reshape(rows, w), d_keys.astype(BF).reshape(rows, w), d_values.astype(BF).reshape(rows, w)],
        axis=1,
    )
    grad_qkv = matmul(normed.T, d_qkv).astype(BF)
    sum_attn = scatter_sum(
        reorder(jnp.concatenate([grad_qkv, grad_out], axis=1), ids[0], n, False), n, orders[0]
    )
    d_normed = swap_sum(matmul_nt(d_qkv, w_qkv))
    scaled = d_normed * gain_one
    d_norm_input = inverse_one * (scaled - normal_one * jnp.mean(scaled * normal_one, axis=-1, keepdims=True))
    grad_gain_one = jnp.sum(d_normed * normal_one, axis=0)

    feed_out = swap_sum(matmul_nt(active, full_down))
    branch = attention + feed_out
    output = (inputs + gate[:, None] * branch).astype(BF)
    d_logit = jnp.sum(upstream * branch, axis=-1) * gate * (1.0 - gate)
    d_router = jnp.sum(d_logit[:, None] * inputs, axis=0)
    d_rows = upstream + d_inner + d_logit[:, None] * router_all.astype(F32) + d_norm_input
    d_rows = d_rows.astype(BF)

    usable_rows = usable.reshape(-1)
    scalars = jnp.stack([jnp.sum(counts).astype(F32), jnp.sum(jnp.where(usable_rows, gate, 0.0))])
    small = jnp.concatenate(
        [
            grad_gain_one.reshape(n, mine),
            grad_gain_two.reshape(n, mine),
            d_router.reshape(n, mine),
            jnp.broadcast_to(scalars, (n, 2)),
        ],
        axis=1,
    )
    small = lax.all_to_all(small, "dp", 0, 0, tiled=True)
    small = jnp.sum(small, axis=0)
    block_out = jnp.stack(
        [sequences[s].at[slots[s]].set(output[s * CAP : (s + 1) * CAP], mode="drop") for s in range(seqs)]
    ).reshape(-1, width)
    input_grad = jnp.stack(
        [upstream_all[s].at[slots[s]].set(d_rows[s * CAP : (s + 1) * CAP], mode="drop") for s in range(seqs)]
    ).reshape(-1, width)
    token_total = tokens_in.shape[0] * n
    return (
        block_out,
        input_grad,
        sum_attn[:, :w],
        sum_attn[:, w : 2 * w],
        sum_attn[:, 2 * w : 3 * w],
        sum_attn[:, 3 * w :].T,
        sum_up,
        sum_down.T,
        small[:mine],
        small[mine : 2 * mine],
        small[2 * mine : 3 * mine],
        small[3 * mine] / token_total,
        small[3 * mine + 1] / small[3 * mine],
    )


def solution(mesh):
    return jax.shard_map(
        body,
        mesh=mesh,
        in_specs=(
            P("dp", None),
            P("dp"),
            P("dp", None),
            P("dp", "mp"),
            P("dp", "mp"),
            P("dp", "mp"),
            P("mp", "dp"),
            P("dp", "mp"),
            P("mp", "dp"),
            P("dp"),
            P("dp"),
            P("dp"),
        ),
        out_specs=(
            P("dp", None),
            P("dp", None),
            P("dp", "mp"),
            P("dp", "mp"),
            P("dp", "mp"),
            P("mp", "dp"),
            P("dp", "mp"),
            P("mp", "dp"),
            P("dp"),
            P("dp"),
            P("dp"),
            P(),
            P(),
        ),
        check_vma=False,
    )
```

time: 1220 us -> 556 us (0.46)
  waiting for transfers between devices: 872 us -> 153 us
  blocking collectives: 100 us -> 0 us
  Pallas kernels: 0 us -> 65.4 us
  local copies, waits for them, and re-layouts: 62.9 us -> 123 us
  starting transfers between devices: 0.85 us -> 46.7 us
  matrix products: 94.6 us -> 53.4 us
  other arithmetic: 62.6 us -> 96.2 us
  between operations: 20.4 us -> 6.99 us
    reduce_scatter x6 -> x0, waiting for transfers between devices: 563 us -> none  [the longest x1 190 us: body(): lax.psum_scatter(mlp_terms[1], 'dp', scatter_dimension=1, tiled=True)]
    all_gather x6 -> x0, waiting for transfers between devices: 256 us -> none  [the longest x1 78.3 us: body(): lax.all_gather(shards[4], 'dp', axis=0, tiled=True)]
    ppermute x0 -> x28, waiting for transfers between devices: none -> 126 us  [the longest x12 68.4 us: gather(): got = lax.ppermute(held, ('dp', 'mp'), pairs(n, one, two))]
    unnamed x2 -> x0, blocking collectives: 97.7 us -> none
    pallas_call x0 -> x6, Pallas kernels: none -> 65.4 us  [reorder(): pl.pallas_call(reorder_kernel, grid_spec=pltpu.PrefetchScalarGridSpec(num...]
    psum x4 -> x0, waiting for transfers between devices: 48.6 us -> none  [the longest x1 20.9 us: block_backward(): lax.psum(part_inner.astype(jnp.bfloat16), 'mp').astype(jnp.float32)]
    ppermute x0 -> x28, starting transfers between devices: none -> 40.3 us  [the longest x12 22.9 us: gather(): got = lax.ppermute(held, ('dp', 'mp'), pairs(n, one, two))]
    dot_general x24 -> x19, matrix products: 88.9 us -> 53.4 us  [the longest x9 27.3 us: matmul(): return jnp.dot(left_side, right_side, preferred_element_type=F32)]
  transfers between devices with their start and end apart: 16 -> 29, of which waited for: 13 -> 10; matrix products, arithmetic and copies ran while one was open for 15% -> 45% of each run, Pallas kernels for 0% -> 10%
where the time goes in v1:
time: 556 us; the launch traced here: 545 us
  waiting for transfers between devices  153 us (28%)
  local copies, waits for them, and re-layouts  123 us (22%)
  other arithmetic  96.2 us (17%)
  Pallas kernels  65.4 us (12%)
  matrix products  53.4 us (10%)
  starting transfers between devices  46.7 us (8%)
  between operations  6.99 us (1%)
    ppermute x12, waiting for transfers between devices, gather(): got = lax.ppermute(held, ('dp', 'mp'), pairs(n, one, two))  68.4 us
    pallas_call x6, Pallas kernels, reorder(): pl.pallas_call(reorder_kernel, grid_spec=pltpu.PrefetchScalarGridSpec(num...  65.4 us
    ppermute x12, waiting for transfers between devices, scatter_sum(): got = lax.ppermute(held[half:], ('dp', 'mp'), pairs(n, one, two))  57.3 us
    scatter-add x2, other arithmetic, compact(): jnp.nonzero(selected, size=CAP, fill_value=LEN)[0].astype(jnp.int32)  29.5 us
    all_to_all x1, waiting for transfers between devices, body(): small = lax.all_to_all(small, 'dp', 0, 0, tiled=True)  27.8 us
    dot_general x9, matrix products, matmul(): return jnp.dot(left_side, right_side, preferred_element_type=F32)  27.3 us
    unnamed x119, local copies, waits for them, and re-layouts  24.3 us
    ppermute x12, starting transfers between devices, gather(): got = lax.ppermute(held, ('dp', 'mp'), pairs(n, one, two))  22.9 us
  transfers between devices with their start and end apart: 29, of which 10 were waited for; matrix products, arithmetic and copies ran while one was open for 45% of the time, Pallas kernels for 10%

profile of v1, /device:TPU:10, one launch (start us, length us, event | category | flops | bytes accessed | tf_op | source)
XLA Modules:
  0.0 545.5 jit_solution(1164901473509287083)
XLA Ops:
  14.1 14.7 %scatter_custom_fusion = s32[256]{0:T(256)S(1)} fusion(s32[2048]{0:T(1024)S(1)} %bitcast.133, s32[2048]{0:T(1024)S(1)} %broadcast.340, s32[]{:T(128)} %constant.106.clone.1), kind=kCustom, calls=%fused_computation.226 | custom fusion | flops 2048 | bytes 1028 | tf_op jit(solution)/shard_map/scatter-add | solution.py:104
  31.1 14.8 %scatter_custom_fusion.1 = s32[256]{0:T(256)S(1)} fusion(s32[2048]{0:T(1024)S(1)} %bitcast.134, s32[2048]{0:T(1024)S(1)} %broadcast.340, s32[]{:T(128)} %constant.106.clone.1), kind=kCustom, calls=%fused_computation.224 | custom fusion | flops 2048 | bytes 1028 | tf_op jit(solution)/shard_map/scatter-add | solution.py:104
  89.7 14.2 %collective-permute-done.1 = bf16[128,2176]{1,0:T(8,128)(2,1)S(1)} collective-permute-done((bf16[128,2176]{1,0:T(8,128)(2,1)}, bf16[128,2176]{1,0:T(8,128)(2,1)S(1)}, u32[]{:S(2)}, u32[]{:S(2)}) %collective-permute-start.1) | collective-permute-done | bytes 557088 | tf_op jit(solution)/shard_map/ppermute | solution.py:57
  106.6 15.2 %collective-permute-done.10 = bf16[128,2048]{1,0:T(8,128)(2,1)S(1)} collective-permute-done((bf16[128,2048]{1,0:T(8,128)(2,1)S(1)}, bf16[128,2048]{1,0:T(8,128)(2,1)S(1)}, u32[]{:S(2)}, u32[]{:S(2)}) %collective-permute-start.10) | collective-permute-done | bytes 524320 | tf_op jit(solution)/shard_map/ppermute | solution.py:57
  140.0 15.5 %collective-permute-done.11 = bf16[256,2048]{1,0:T(8,128)(2,1)S(1)} collective-permute-done((bf16[256,2048]{1,0:T(8,128)(2,1)S(1)}, bf16[256,2048]{1,0:T(8,128)(2,1)S(1)}, u32[]{:S(2)}, u32[]{:S(2)}) %collective-permute-start.11) | collective-permute-done | bytes 1048608 | tf_op jit(solution)/shard_map/ppermute | solution.py:57
  158.5 19.4 %collective-permute-done.7 = bf16[256,2048]{1,0:T(8,128)(2,1)S(1)} collective-permute-done((bf16[256,2048]{1,0:T(8,128)(2,1)S(1)}, bf16[256,2048]{1,0:T(8,128)(2,1)S(1)}, u32[]{:S(2)}, u32[]{:S(2)}) %collective-permute-start.7) | collective-permute-done | bytes 1048608 | tf_op jit(solution)/shard_map/ppermute | solution.py:57
  185.6 11.1 %shard_map.273 = bf16[1024,2176]{1,0:T(8,128)(2,1)} custom-call(s32[16]{0:T(128)} %fusion.76.ids_ref, bf16[1024,2176]{1,0:T(8,128)(2,1)} %constant_dynamic-update-slice_fusion.in_ref), custom_call_target="tpu_custom_call" | custom-call | bytes 8912896 | tf_op jit(solution)/shard_map/pallas_call | solution.py:90
  224.6 10.8 %shard_map.275 = bf16[1024,2048]{1,0:T(8,128)(2,1)} custom-call(s32[16]{0:T(128)} %fusion.77.ids_ref, bf16[1024,2048]{1,0:T(8,128)(2,1)} %constant_dynamic-update-slice_fusion.10.in_ref), custom_call_target="tpu_custom_call" | custom-call | bytes 8388608 | tf_op jit(solution)/shard_map/pallas_call | solution.py:90
  238.6 10.8 %shard_map.274 = bf16[1024,2048]{1,0:T(8,128)(2,1)} custom-call(s32[16]{0:T(128)} %fusion.77.ids_ref, bf16[1024,2048]{1,0:T(8,128)(2,1)} %constant_dynamic-update-slice_fusion.5.in_ref), custom_call_target="tpu_custom_call" | custom-call | bytes 8388608 | tf_op jit(solution)/shard_map/pallas_call | solution.py:90
  273.1 10.8 %shard_map.278 = bf16[1024,2048]{1,0:T(8,128)(2,1)} custom-call(s32[16]{0:T(128)} %fusion.77.ids_ref, bf16[1024,2048]{1,0:T(8,128)(2,1)} %convolution_convert_fusion.in_ref), custom_call_target="tpu_custom_call" | custom-call | bytes 8388608 | tf_op jit(solution)/shard_map/pallas_call | solution.py:90
  284.1 7.3 %convolution_convert_fusion.7 = bf16[512,1024]{1,0:T(8,128)(2,1)} fusion(bf16[1024,2048]{1,0:T(8,128)(2,1)} %shard_map.275, f32[512,2048]{1,0:T(8,128)} %copy-done.46), kind=kOutput, calls=%fused_computation.91 | convolution fusion | flops 2157445120 | bytes 9437184 | tf_op jit(solution)/shard_map/dot_general | solution.py:24
  297.8 10.8 %shard_map.277 = bf16[1024,2048]{1,0:T(8,128)(2,1)} custom-call(s32[16]{0:T(128)} %fusion.77.ids_ref, bf16[1024,2048]{1,0:T(8,128)(2,1)} %convolution_convert_fusion.1.in_ref), custom_call_target="tpu_custom_call" | custom-call | bytes 8388608 | tf_op jit(solution)/shard_map/pallas_call | solution.py:90
  335.5 7.0 %scatter_custom_fusion.3 = bf16[2048,1024]{1,0:T(8,128)(2,1)} fusion(bf16[2048,1024]{1,0:T(8,128)(2,1)} %get-tuple-element.38, s32[256]{0:T(256)S(1)} %bitcast.140, bf16[512,1024]{1,0:T(8,128)(2,1)} %get-tuple-element.40), kind=kCustom, calls=%fused_computation.120 | custom fusion | bytes 4718592 | tf_op jit(solution)/shard_map/scatter | solution.py:247
  342.5 7.2 %scatter_custom_fusion.2 = bf16[2048,1024]{1,0:T(8,128)(2,1)} fusion(bf16[2048,1024]{1,0:T(8,128)(2,1)} %get-tuple-element.37, s32[256]{0:T(256)S(1)} %bitcast.138, bf16[512,1024]{1,0:T(8,128)(2,1)} %get-tuple-element.40), kind=kCustom, calls=%fused_computation.122 | custom fusion | bytes 4718592 | tf_op jit(solution)/shard_map/scatter | solution.py:247
  371.8 11.1 %shard_map.276 = bf16[1024,2048]{1,0:T(8,128)(2,1)} custom-call(s32[16]{0:T(128)} %fusion.76.ids_ref, bf16[1024,2048]{1,0:T(8,128)(2,1)} %pad_maximum_fusion.2.in_ref), custom_call_target="tpu_custom_call" | custom-call | bytes 8388608 | tf_op jit(solution)/shard_map/pallas_call | solution.py:90
  394.0 7.1 %scatter_custom_fusion.5 = bf16[2048,1024]{1,0:T(8,128)(2,1)} fusion(bf16[2048,1024]{1,0:T(8,128)(2,1)} %get-tuple-element.36, s32[256]{0:T(256)S(1)} %bitcast.141, bf16[512,1024]{1,0:T(8,128)(2,1)} %fusion.21), kind=kCustom, calls=%fused_computation.116 | custom fusion | bytes 4718592 | tf_op jit(solution)/shard_map/scatter | solution.py:250
  401.1 6.5 %scatter_custom_fusion.4 = bf16[2048,1024]{1,0:T(8,128)(2,1)} fusion(bf16[2048,1024]{1,0:T(8,128)(2,1)} %get-tuple-element.35, s32[256]{0:T(256)S(1)} %bitcast.139, bf16[512,1024]{1,0:T(8,128)(2,1)S(1)} %copy-done.26), kind=kCustom, calls=%fused_computation.118 | custom fusion | bytes 4718592 | tf_op jit(solution)/shard_map/scatter | solution.py:250
  419.9 6.4 %all-to-all-start = ((f32[16,1,194]{2,1,0:T(1,128)}), f32[16,1,194]{2,1,0:T(1,128)S(1)}, u32[]{:S(2)}, u32[]{:S(2)}) async-start(f32[16,1,194]{2,1,0:T(1,128)} %all_to_all.6), calls=%async_computation | async-start | bytes 32768 | tf_op jit(solution)/shard_map/all_to_all | solution.py:244
  426.3 7.6 %pad_maximum_fusion.1 = bf16[2,2048,1024]{2,1,0:T(8,128)(2,1)} fusion(bf16[1,2048,1024]{2,1,0:T(8,128)(2,1)} %bitcast.112, bf16[1,2048,1024]{2,1,0:T(8,128)(2,1)} %bitcast.111), kind=kLoop, calls=%fused_computation.12 | loop fusion | flops 4194304 | bytes 16777216 | tf_op jit(solution)/shard_map/stack | solution.py:249
  433.9 27.8 %all-to-all-done = f32[16,1,194]{2,1,0:T(1,128)S(1)} async-done(((f32[16,1,194]{2,1,0:T(1,128)}), f32[16,1,194]{2,1,0:T(1,128)S(1)}, u32[]{:S(2)}, u32[]{:S(2)}) %all-to-all-start) | async-done | bytes 12448 | tf_op jit(solution)/shard_map/all_to_all | solution.py:244
  474.4 31.1 %collective-permute-done.22 = bf16[128,2048]{1,0:T(8,128)(2,1)S(1)} collective-permute-done((bf16[128,2048]{1,0:T(8,128)(2,1)S(1)}, bf16[128,2048]{1,0:T(8,128)(2,1)S(1)}, u32[]{:S(2)}, u32[]{:S(2)}) %collective-permute-start.22) | collective-permute-done | bytes 524320 | tf_op jit(solution)/shard_map/ppermute | solution.py:67
  509.4 7.3 %collective-permute-done.26 = bf16[128,2048]{1,0:T(8,128)(2,1)S(1)} collective-permute-done((bf16[128,2048]{1,0:T(8,128)(2,1)S(1)}, bf16[128,2048]{1,0:T(8,128)(2,1)S(1)}, u32[]{:S(2)}, u32[]{:S(2)}) %collective-permute-start.26) | collective-permute-done | bytes 524320 | tf_op jit(solution)/shard_map/ppermute | solution.py:67
  518.5 9.4 %collective-permute-done.18 = bf16[128,2048]{1,0:T(8,128)(2,1)S(1)} collective-permute-done((bf16[128,2048]{1,0:T(8,128)(2,1)S(1)}, bf16[128,2048]{1,0:T(8,128)(2,1)S(1)}, u32[]{:S(2)}, u32[]{:S(2)}) %collective-permute-start.18) | collective-permute-done | bytes 524320 | tf_op jit(solution)/shard_map/ppermute | solution.py:67
  532.4 9.5 %collective-permute-done.19 = bf16[64,2048]{1,0:T(8,128)(2,1)S(1)} collective-permute-done((bf16[64,2048]{1,0:T(8,128)(2,1)S(1)}, bf16[64,2048]{1,0:T(8,128)(2,1)S(1)}, u32[]{:S(2)}, u32[]{:S(2)}) %collective-permute-start.19) | collective-permute-done | bytes 262176 | tf_op jit(solution)/shard_map/ppermute | solution.py:67
  (311 shorter events, 245.1 us)
Async XLA Ops:
  0.6 85.8 %collective-permute-start.9 = (bf16[64,2048]{1,0:T(8,128)(2,1)}, bf16[64,2048]{1,0:T(8,128)(2,1)S(1)}, u32[]{:S(2)}, u32[]{:S(2)}) collective-permute-start(bf16[64,2048]{1,0:T(8,128)(2,1)} %bitcast.117), channel_id=1, source_target_pairs={{0,2},{1,5},{2,0},{3,7},{4,6},{5,1},{6,4},{7,3},{8,10},{9,13},{10,... | collective-permute-start | bytes 786440 | tf_op jit(solution)/shard_map/ppermute | solution.py:57
  1.2 85.7 %collective-permute-start.5 = (bf16[64,2048]{1,0:T(8,128)(2,1)}, bf16[64,2048]{1,0:T(8,128)(2,1)S(1)}, u32[]{:S(2)}, u32[]{:S(2)}) collective-permute-start(bf16[64,2048]{1,0:T(8,128)(2,1)} %param.27), channel_id=1, source_target_pairs={{0,2},{1,5},{2,0},{3,7},{4,6},{5,1},{6,4},{7,3},{8,10},{9,13},{10,... | collective-permute-start | bytes 786440 | tf_op jit(solution)/shard_map/ppermute | solution.py:57
  6.1 77.3 %collective-permute-start = (bf16[64,2176]{1,0:T(8,128)(2,1)S(1)}, bf16[64,2176]{1,0:T(8,128)(2,1)S(1)}, u32[]{:S(2)}, u32[]{:S(2)}) collective-permute-start(bf16[64,2176]{1,0:T(8,128)(2,1)S(1)} %concatenate.64), channel_id=1, source_target_pairs={{0,16},{1,17},{2,18},{3,19},{4,20},{5,21},{6,22},{7,23},{8,24},{9,... | collective-permute-start | bytes 835592 | tf_op jit(solution)/shard_map/ppermute | solution.py:57
  86.5 35.3 %collective-permute-start.10 = (bf16[128,2048]{1,0:T(8,128)(2,1)S(1)}, bf16[128,2048]{1,0:T(8,128)(2,1)S(1)}, u32[]{:S(2)}, u32[]{:S(2)}) collective-permute-start(bf16[128,2048]{1,0:T(8,128)(2,1)S(1)} %pad_maximum_fusion.13), channel_id=1, source_target_pairs={{0,16},{1,17},{2,18},{3,19},{4,20},{5,21},{6,22},{7,23},{8,24},{9,... | collective-permute-start | bytes 1572872 | tf_op jit(solution)/shard_map/ppermute | solution.py:57
  87.0 43.8 %collective-permute-start.6 = (bf16[128,2048]{1,0:T(8,128)(2,1)S(1)}, bf16[128,2048]{1,0:T(8,128)(2,1)S(1)}, u32[]{:S(2)}, u32[]{:S(2)}) collective-permute-start(bf16[128,2048]{1,0:T(8,128)(2,1)S(1)} %pad_maximum_fusion.12), channel_id=1, source_target_pairs={{0,16},{1,17},{2,18},{3,19},{4,20},{5,21},{6,22},{7,23},{8,24},{9,... | collective-permute-start | bytes 1572872 | tf_op jit(solution)/shard_map/ppermute | solution.py:57
  103.9 31.8 %collective-permute-start.2 = (bf16[256,2176]{1,0:T(8,128)(2,1)S(1)}, bf16[256,2176]{1,0:T(8,128)(2,1)S(1)}, u32[]{:S(2)}, u32[]{:S(2)}) collective-permute-start(bf16[256,2176]{1,0:T(8,128)(2,1)S(1)} %pad_maximum_fusion.6), channel_id=1, source_target_pairs={{0,2},{1,5},{2,0},{3,7},{4,6},{5,1},{6,4},{7,3},{8,10},{9,13},{10,... | collective-permute-start | bytes 3342344 | tf_op jit(solution)/shard_map/ppermute | solution.py:57
  122.0 33.5 %collective-permute-start.11 = (bf16[256,2048]{1,0:T(8,128)(2,1)S(1)}, bf16[256,2048]{1,0:T(8,128)(2,1)S(1)}, u32[]{:S(2)}, u32[]{:S(2)}) collective-permute-start(bf16[256,2048]{1,0:T(8,128)(2,1)S(1)} %pad_maximum_fusion.9), channel_id=1, source_target_pairs={{0,8},{1,9},{2,10},{3,11},{4,12},{5,13},{6,14},{7,15},{8,0},{9,1},... | collective-permute-start | bytes 3145736 | tf_op jit(solution)/shard_map/ppermute | solution.py:57
  130.9 46.9 %collective-permute-start.7 = (bf16[256,2048]{1,0:T(8,128)(2,1)S(1)}, bf16[256,2048]{1,0:T(8,128)(2,1)S(1)}, u32[]{:S(2)}, u32[]{:S(2)}) collective-permute-start(bf16[256,2048]{1,0:T(8,128)(2,1)S(1)} %pad_maximum_fusion.8), channel_id=1, source_target_pairs={{0,8},{1,9},{2,10},{3,11},{4,12},{5,13},{6,14},{7,15},{8,0},{9,1},... | collective-permute-start | bytes 3145736 | tf_op jit(solution)/shard_map/ppermute | solution.py:57
  135.8 48.3 %collective-permute-start.3 = (bf16[512,2176]{1,0:T(8,128)(2,1)S(1)}, bf16[512,2176]{1,0:T(8,128)(2,1)S(1)}, u32[]{:S(2)}, u32[]{:S(2)}) collective-permute-start(bf16[512,2176]{1,0:T(8,128)(2,1)S(1)} %pad_maximum_fusion.3), channel_id=1, source_target_pairs={{0,4},{1,3},{2,6},{3,1},{4,0},{5,7},{6,2},{7,5},{8,12},{9,11},{10,... | collective-permute-start | bytes 6684680 | tf_op jit(solution)/shard_map/ppermute | solution.py:57
  157.0 64.2 %collective-permute-start.12 = (bf16[512,2048]{1,0:T(8,128)(2,1)}, bf16[512,2048]{1,0:T(8,128)(2,1)}, u32[]{:S(2)}, u32[]{:S(2)}) collective-permute-start(bf16[512,2048]{1,0:T(8,128)(2,1)} %pad_maximum_fusion.5), channel_id=1, source_target_pairs={{0,4},{1,3},{2,6},{3,1},{4,0},{5,7},{6,2},{7,5},{8,12},{9,11},{10,... | collective-permute-start | bytes 6291464 | tf_op jit(solution)/shard_map/ppermute | solution.py:57
  179.3 56.1 %collective-permute-start.8 = (bf16[512,2048]{1,0:T(8,128)(2,1)}, bf16[512,2048]{1,0:T(8,128)(2,1)}, u32[]{:S(2)}, u32[]{:S(2)}) collective-permute-start(bf16[512,2048]{1,0:T(8,128)(2,1)} %pad_maximum_fusion.4), channel_id=1, source_target_pairs={{0,4},{1,3},{2,6},{3,1},{4,0},{5,7},{6,2},{7,5},{8,12},{9,11},{10,... | collective-permute-start | bytes 6291464 | tf_op jit(solution)/shard_map/ppermute | solution.py:57
  221.1 31.4 %collective-permute-start.4 = (bf16[512,1024]{1,0:T(8,128)(2,1)S(1)}, bf16[512,1024]{1,0:T(8,128)(2,1)}, u32[]{:S(2)}, u32[]{:S(2)}) collective-permute-start(bf16[512,1024]{1,0:T(8,128)(2,1)S(1)} %convolution_convert_fusion.5), channel_id=1, source_target_pairs={{0,1},{1,0},{2,3},{3,2},{4,5},{5,4},{6,7},{7,6},{8,9},{9,8},{10,11... | collective-permute-start | bytes 3145736 | tf_op jit(solution)/shard_map/ppermute | solution.py:111
  283.9 30.1 %collective-permute-start.14 = (bf16[512,1024]{1,0:T(8,128)(2,1)}, bf16[512,1024]{1,0:T(8,128)(2,1)}, u32[]{:S(2)}, u32[]{:S(2)}) collective-permute-start(bf16[512,1024]{1,0:T(8,128)(2,1)} %convolution_convert_fusion.6), channel_id=1, source_target_pairs={{0,1},{1,0},{2,3},{3,2},{4,5},{5,4},{6,7},{7,6},{8,9},{9,8},{10,11... | collective-permute-start | bytes 3145736 | tf_op jit(solution)/shard_map/ppermute | solution.py:111
  291.3 24.7 %collective-permute-start.13 = (bf16[512,1024]{1,0:T(8,128)(2,1)}, bf16[512,1024]{1,0:T(8,128)(2,1)}, u32[]{:S(2)}, u32[]{:S(2)}) collective-permute-start(bf16[512,1024]{1,0:T(8,128)(2,1)} %convolution_convert_fusion.7), channel_id=1, source_target_pairs={{0,1},{1,0},{2,3},{3,2},{4,5},{5,4},{6,7},{7,6},{8,9},{9,8},{10,11... | collective-permute-start | bytes 3145736 | tf_op jit(solution)/shard_map/ppermute | solution.py:111
  311.9 95.7 %collective-permute-start.20 = (bf16[512,2048]{1,0:T(8,128)(2,1)}, bf16[512,2048]{1,0:T(8,128)(2,1)}, u32[]{:S(2)}, u32[]{:S(2)}) collective-permute-start(bf16[512,2048]{1,0:T(8,128)(2,1)} %slice.308), channel_id=1, source_target_pairs={{0,4},{1,3},{2,6},{3,1},{4,0},{5,7},{6,2},{7,5},{8,12},{9,11},{10,... | collective-permute-start | bytes 6291464 | tf_op jit(solution)/shard_map/ppermute | solution.py:67
  312.5 101.9 %collective-permute-start.24 = (bf16[512,2048]{1,0:T(8,128)(2,1)}, bf16[512,2048]{1,0:T(8,128)(2,1)}, u32[]{:S(2)}, u32[]{:S(2)}) collective-permute-start(bf16[512,2048]{1,0:T(8,128)(2,1)} %slice.316), channel_id=1, source_target_pairs={{0,4},{1,3},{2,6},{3,1},{4,0},{5,7},{6,2},{7,5},{8,12},{9,11},{10,... | collective-permute-start | bytes 6291464 | tf_op jit(solution)/shard_map/ppermute | solution.py:67
  358.3 28.2 %collective-permute-start.15 = (bf16[512,1024]{1,0:T(8,128)(2,1)}, bf16[512,1024]{1,0:T(8,128)(2,1)}, u32[]{:S(2)}, u32[]{:S(2)}) collective-permute-start(bf16[512,1024]{1,0:T(8,128)(2,1)} %fusion.36), channel_id=1, source_target_pairs={{0,1},{1,0},{2,3},{3,2},{4,5},{5,4},{6,7},{7,6},{8,9},{9,8},{10,11... | collective-permute-start | bytes 3145736 | tf_op jit(solution)/shard_map/ppermute | solution.py:111
  386.1 78.8 %collective-permute-start.16 = (bf16[512,2048]{1,0:T(8,128)(2,1)}, bf16[512,2048]{1,0:T(8,128)(2,1)}, u32[]{:S(2)}, u32[]{:S(2)}) collective-permute-start(bf16[512,2048]{1,0:T(8,128)(2,1)} %slice.296), channel_id=1, source_target_pairs={{0,4},{1,3},{2,6},{3,1},{4,0},{5,7},{6,2},{7,5},{8,12},{9,11},{10,... | collective-permute-start | bytes 6291464 | tf_op jit(solution)/shard_map/ppermute | solution.py:67
  411.9 57.4 %collective-permute-start.21 = (bf16[256,2048]{1,0:T(8,128)(2,1)}, bf16[256,2048]{1,0:T(8,128)(2,1)S(1)}, u32[]{:S(2)}, u32[]{:S(2)}) collective-permute-start(bf16[256,2048]{1,0:T(8,128)(2,1)} %slice.310), channel_id=1, source_target_pairs={{0,8},{1,9},{2,10},{3,11},{4,12},{5,13},{6,14},{7,15},{8,0},{9,1},... | collective-permute-start | bytes 3145736 | tf_op jit(solution)/shard_map/ppermute | solution.py:67
  419.1 53.1 %collective-permute-start.25 = (bf16[256,2048]{1,0:T(8,128)(2,1)}, bf16[256,2048]{1,0:T(8,128)(2,1)}, u32[]{:S(2)}, u32[]{:S(2)}) collective-permute-start(bf16[256,2048]{1,0:T(8,128)(2,1)} %slice.318), channel_id=1, source_target_pairs={{0,8},{1,9},{2,10},{3,11},{4,12},{5,13},{6,14},{7,15},{8,0},{9,1},... | collective-permute-start | bytes 3145736 | tf_op jit(solution)/shard_map/ppermute | solution.py:67
  419.9 41.8 %all-to-all-start = ((f32[16,1,194]{2,1,0:T(1,128)}), f32[16,1,194]{2,1,0:T(1,128)S(1)}, u32[]{:S(2)}, u32[]{:S(2)}) async-start(f32[16,1,194]{2,1,0:T(1,128)} %all_to_all.6), calls=%async_computation | async-start | bytes 32768 | tf_op jit(solution)/shard_map/all_to_all | solution.py:244
  468.0 38.4 %collective-permute-start.17 = (bf16[256,2048]{1,0:T(8,128)(2,1)S(1)}, bf16[256,2048]{1,0:T(8,128)(2,1)S(1)}, u32[]{:S(2)}, u32[]{:S(2)}) collective-permute-start(bf16[256,2048]{1,0:T(8,128)(2,1)S(1)} %slice.298), channel_id=1, source_target_pairs={{0,2},{1,5},{2,0},{3,7},{4,6},{5,1},{6,4},{7,3},{8,10},{9,13},{10,... | collective-permute-start | bytes 3145736 | tf_op jit(solution)/shard_map/ppermute | solution.py:67
  469.7 35.8 %collective-permute-start.22 = (bf16[128,2048]{1,0:T(8,128)(2,1)S(1)}, bf16[128,2048]{1,0:T(8,128)(2,1)S(1)}, u32[]{:S(2)}, u32[]{:S(2)}) collective-permute-start(bf16[128,2048]{1,0:T(8,128)(2,1)S(1)} %slice.312), channel_id=1, source_target_pairs={{0,16},{1,17},{2,18},{3,19},{4,20},{5,21},{6,22},{7,23},{8,24},{9,... | collective-permute-start | bytes 1572872 | tf_op jit(solution)/shard_map/ppermute | solution.py:67
  473.8 42.9 %collective-permute-start.26 = (bf16[128,2048]{1,0:T(8,128)(2,1)S(1)}, bf16[128,2048]{1,0:T(8,128)(2,1)S(1)}, u32[]{:S(2)}, u32[]{:S(2)}) collective-permute-start(bf16[128,2048]{1,0:T(8,128)(2,1)S(1)} %slice.320), channel_id=1, source_target_pairs={{0,16},{1,17},{2,18},{3,19},{4,20},{5,21},{6,22},{7,23},{8,24},{9,... | collective-permute-start | bytes 1572872 | tf_op jit(solution)/shard_map/ppermute | solution.py:67
  (54 other events, 656.3 us)
